TPU v7x, 32 devices: a whole 2x2x4 slice. The times are simulated.
32 devices in a mesh: blk: 4 (over y, core), ctx: 4 (over z), tp: 2 (over x).
Axes of the slice: x: 2, y: 2, z: 4, core: 2. Of those that a mesh axis runs over, the one named last changes fastest.
Arguments:
- query_proj: bfloat16 [2048, 4096], P(('blk', 'ctx'), 'tp'), may hold values from -6 to 6
- key_proj: bfloat16 [2048, 4096], P(('blk', 'ctx'), 'tp'), may hold values from -30 to 30
- value_proj: bfloat16 [2048, 4096], P(('blk', 'ctx'), 'tp'), may hold values from -6 to 6
- output_grad: bfloat16 [2048, 4096], P(('blk', 'ctx'), 'tp'), may hold values from -6 to 6
- long_filter: float32 [2, 2048, 2048], P('tp', ('blk', 'ctx')), may hold values from -0.6 to 0.6
Outputs:
- query_grad: bfloat16 [2048, 4096], P(('blk', 'ctx'), 'tp')
- key_grad: bfloat16 [2048, 4096], P(('blk', 'ctx'), 'tp')
- value_grad: bfloat16 [2048, 4096], P(('blk', 'ctx'), 'tp')
- filter_grad: float32 [2, 2048, 2048], P('tp', ('blk', 'ctx'))
All inputs are finite; a program needn't handle non-finite values.
Results may differ from a plain program's by a relative error of at most 0.0085.
Values may be sent and summed in bfloat16 or wider, within the bound.
A program may use at most 128 MiB of HBM per device.

v0:
```python
import functools
import math

import jax
import jax.numpy as jnp
import ml_dtypes
import numpy as np
from jax import lax
from jax.experimental import pallas as pl
from jax.experimental.pallas import tpu as pltpu
from jax.sharding import PartitionSpec as P

PRECISE = lax.Precision.HIGH
MESH = pl.DeviceIdType.MESH
TILE = 128
CHUNK = 16
F32 = jnp.float32
BF16 = jnp.bfloat16


def spectrum_tables(seq_length):
    outer_size = seq_length // 64
    half_size = outer_size // 2
    full_size = outer_size * 128
    row_index = lax.broadcasted_iota(jnp.int32, (outer_size, half_size), 0)
    col_index = lax.broadcasted_iota(jnp.int32, (outer_size, half_size), 1)
    outer_angle = (row_index * col_index % outer_size).astype(jnp.float32) * (
        2.0 * math.pi / outer_size
    )
    inner_row = lax.broadcasted_iota(jnp.int32, (128, 128), 0)
    inner_col = lax.broadcasted_iota(jnp.int32, (128, 128), 1)
    inner_angle = (inner_row * inner_col % 128).astype(jnp.float32) * (2.0 * math.pi / 128)
    twist_row = lax.broadcasted_iota(jnp.int32, (outer_size, 128), 0)
    twist_col = lax.broadcasted_iota(jnp.int32, (outer_size, 128), 1)
    twist_angle = (twist_row * twist_col % full_size).astype(jnp.float32) * (
        2.0 * math.pi / full_size
    )
    return (
        jnp.cos(outer_angle),
        jnp.sin(outer_angle),
        jnp.cos(inner_angle),
        jnp.sin(inner_angle),
        jnp.cos(twist_angle),
        jnp.sin(twist_angle),
        full_size,
    )


def to_spectrum(signal, tables):
    outer_cos, outer_sin, inner_cos, inner_sin, twist_cos, twist_sin, full_size = tables
    blocks = signal.reshape(signal.shape[0], outer_cos.shape[1], 128)
    first_real = jnp.einsum("kn,cnm->ckm", outer_cos, blocks, precision=PRECISE)
    first_imag = -jnp.einsum("kn,cnm->ckm", outer_sin, blocks, precision=PRECISE)
    turned_real = first_real * twist_cos + first_imag * twist_sin
    turned_imag = first_imag * twist_cos - first_real * twist_sin
    real_part = jnp.einsum("ckm,mj->ckj", turned_real, inner_cos, precision=PRECISE) + jnp.einsum(
        "ckm,mj->ckj", turned_imag, inner_sin, precision=PRECISE
    )
    imag_part = jnp.einsum("ckm,mj->ckj", turned_imag, inner_cos, precision=PRECISE) - jnp.einsum(
        "ckm,mj->ckj", turned_real, inner_sin, precision=PRECISE
    )
    return (real_part, imag_part)


def from_spectrum(spectrum, tables):
    outer_cos, outer_sin, inner_cos, inner_sin, twist_cos, twist_sin, full_size = tables
    real_part, imag_part = spectrum
    mixed_real = jnp.einsum("ckm,mj->ckj", real_part, inner_cos, precision=PRECISE) - jnp.einsum(
        "ckm,mj->ckj", imag_part, inner_sin, precision=PRECISE
    )
    mixed_imag = jnp.einsum("ckm,mj->ckj", imag_part, inner_cos, precision=PRECISE) + jnp.einsum(
        "ckm,mj->ckj", real_part, inner_sin, precision=PRECISE
    )
    turned_real = mixed_real * twist_cos - mixed_imag * twist_sin
    turned_imag = mixed_imag * twist_cos + mixed_real * twist_sin
    signal = jnp.einsum("kn,ckm->cnm", outer_cos, turned_real, precision=PRECISE) - jnp.einsum(
        "kn,ckm->cnm", outer_sin, turned_imag, precision=PRECISE
    )
    return (signal / full_size).reshape(signal.shape[0], -1)


def complex_product(left, right, conjugate):
    left_real, left_imag = left
    right_real, right_imag = right
    if conjugate:
        return (
            left_real * right_real + left_imag * right_imag,
            left_imag * right_real - left_real * right_imag,
        )
    return (
        left_real * right_real - left_imag * right_imag,
        left_real * right_imag + left_imag * right_real,
    )


def channel_work(gated_cols, gate_cols, kernel_cols):
    tables = spectrum_tables(kernel_cols.shape[1])
    kernel_spec = to_spectrum(kernel_cols, tables)
    gated_spec = to_spectrum(gated_cols.astype(jnp.float32), tables)
    gate_spec = to_spectrum(gate_cols.astype(jnp.float32), tables)
    conv_out = from_spectrum(complex_product(gated_spec, kernel_spec, False), tables).astype(
        jnp.bfloat16
    )
    conv_grad = from_spectrum(complex_product(gate_spec, kernel_spec, True), tables).astype(
        jnp.bfloat16
    )
    filter_raw = from_spectrum(complex_product(gate_spec, gated_spec, True), tables)
    return (conv_out, conv_grad, filter_raw)


def gated_product(left, right):
    return (left.astype(jnp.float32) * right.astype(jnp.float32)).astype(jnp.bfloat16)


def turn(value, step, span):
    re, im = value
    step = step % span
    if step == 0:
        return value
    if 4 * step == span:
        return (im, -re)
    if 2 * step == span:
        return (-re, -im)
    if 4 * step == 3 * span:
        return (-im, re)
    c = math.cos(2.0 * math.pi * step / span)
    s = math.sin(2.0 * math.pi * step / span)
    if (8 * step) % span == 0:
        r = abs(c)
        a, b = r * (re + im), r * (im - re)
        eighth = 8 * step // span
        return {1: (a, b), 3: (b, -a), 5: (-a, -b), 7: (-b, a)}[eighth]
    return (c * re + s * im, c * im - s * re)


def complex_dft(values, way):
    n = len(values)
    if n == 1:
        return values
    even = complex_dft(values[0::2], way)
    odd = complex_dft(values[1::2], way)
    out = [None] * n
    for k in range(n // 2):
        tr, ti = turn(odd[k], way * k, n)
        er, ei = even[k]
        out[k] = (er + tr, ei + ti)
        out[k + n // 2] = (er - tr, ei - ti)
    return out


def odd_bins(d, span):
    q = span // 4
    z = [turn((d[n], -d[n + q]), n, span) for n in range(q)]
    out = {}
    for m, (re, im) in enumerate(complex_dft(z, 1)):
        k = 4 * m + 1
        if k < span // 2:
            out[k] = (re, im)
        else:
            out[span - k] = (re, -im)
    return out


def real_bins(x):
    n = len(x)
    if n == 1:
        return {0: (x[0], None)}
    h = n // 2
    out = {2 * k: v for k, v in real_bins([x[i] + x[i + h] for i in range(h)]).items()}
    d = [x[i] - x[i + h] for i in range(h)]
    if n == 2:
        out[1] = (d[0], None)
    else:
        out.update(odd_bins(d, n))
    return out


def padded_bins(x):
    out = {2 * k: v for k, v in real_bins(x).items()}
    out.update(odd_bins(x, 2 * len(x)))
    return out


def odd_back(bins, span):
    q = span // 4
    c = []
    for m in range(q):
        k = 4 * m + 1
        if k < span // 2:
            c.append(bins[k])
        else:
            re, im = bins[span - k]
            c.append((re, -im))
    w = [turn(v, -n, span) for n, v in enumerate(complex_dft(c, -1))]
    return [v[0] for v in w] + [-v[1] for v in w]


def real_back(bins, n):
    if n == 1:
        return [bins[0][0]]
    if n == 2:
        return [bins[0][0] + bins[1][0], bins[0][0] - bins[1][0]]
    h = n // 2
    e = real_back({k // 2: bins[k] for k in bins if k % 2 == 0}, h)
    o = odd_back({k: bins[k] for k in bins if k % 2 == 1}, n)
    return [a + b for a, b in zip(e, o)] + [a - b for a, b in zip(e, o)]


def padded_back(bins, n):
    e = real_back({k // 2: bins[k] for k in bins if k % 2 == 0}, n)
    o = odd_back({k: bins[k] for k in bins if k % 2 == 1}, 2 * n)
    return [a + b for a, b in zip(e, o)]


def inner_tables(blocks):
    span = 2 * blocks
    full = span * TILE
    k1 = np.arange(blocks + 1).reshape(-1, 1, 1)
    k2 = np.arange(TILE).reshape(1, -1, 1)
    n2 = np.arange(TILE).reshape(1, 1, -1)
    angle = (n2 * (k1 + span * k2) % full) * (2.0 * math.pi / full)
    c, s = np.cos(angle), np.sin(angle)
    fwd = np.concatenate(
        [np.concatenate([c, s], 2), np.concatenate([-s, c], 2)], 1
    )
    weight = np.where((k1 == 0) | (k1 == blocks), 1.0, 2.0) / full
    inv = fwd.transpose(0, 2, 1) * weight

    def parts(m):
        hi = m.astype(ml_dtypes.bfloat16)
        lo = (m - hi.astype(np.float64)).astype(ml_dtypes.bfloat16)
        return np.concatenate([hi, lo], 1)

    return parts(fwd), parts(inv)


def fused_kernel(
    cfg,
    k_ref, v_ref, q_ref, og_ref, filt_ref, fwd_hbm, inv_hbm,
    co_ref, cg_ref, raw_ref, fac_ref,
    fwd, inv, send, recv, outer, spec_f, spec_kv, spec_gg, back, wide,
    sq_mine, sq_tp, sq_pair, sq_all,
    table_sem, send_sem, recv_sem, sq_send, sq_recv, tp_send, tp_recv,
):
    blocks, n_ctx, n_tp, entries = cfg
    me = lax.axis_index("blk") * n_ctx + lax.axis_index("ctx")
    my_tp = lax.axis_index("tp")
    bins = blocks + 1

    def place(d):
        return {"blk": d // n_ctx, "ctx": d % n_ctx}

    get_fwd = pltpu.make_async_copy(fwd_hbm, fwd, table_sem.at[0])
    get_inv = pltpu.make_async_copy(inv_hbm, inv, table_sem.at[1])
    get_fwd.start()
    get_inv.start()

    barrier = pltpu.get_barrier_semaphore()

    def greet(j, carry):
        d = lax.rem(me + j, blocks)
        pl.semaphore_signal(barrier, inc=1, device_id=place(d), device_id_type=MESH)
        return carry

    lax.fori_loop(1, blocks, greet, 0)
    for j in range(1, n_tp):
        pl.semaphore_signal(
            barrier, inc=1, device_id={"tp": lax.rem(my_tp + j, n_tp)}, device_id_type=MESH
        )

    def gate(phase, a_ref, b_ref):
        for d in range(blocks):
            cols = slice(d * TILE, (d + 1) * TILE)
            send[phase, d] = gated_product(a_ref[:, cols], b_ref[:, cols])
        recv[phase, me] = send[phase, me]

    def out_copy(phase, d):
        return pltpu.make_async_remote_copy(
            src_ref=send.at[phase, d],
            dst_ref=recv.at[phase, me],
            send_sem=send_sem.at[phase, d],
            recv_sem=recv_sem.at[phase, me],
            device_id=place(d),
            device_id_type=MESH,
        )

    def in_copy(phase, s):
        return pltpu.make_async_remote_copy(
            src_ref=send.at[phase, s],
            dst_ref=recv.at[phase, s],
            send_sem=send_sem.at[phase, s],
            recv_sem=recv_sem.at[phase, s],
            device_id=place(s),
            device_id_type=MESH,
        )

    def start_all(phase):
        def one(j, carry):
            out_copy(phase, lax.rem(me + j, blocks)).start()
            return carry

        lax.fori_loop(1, blocks, one, 0)

    def arrive_all(phase):
        def one(j, carry):
            in_copy(phase, lax.rem(me + blocks - j, blocks)).wait_recv()
            return carry

        lax.fori_loop(1, blocks, one, 0)

    def rows_at(i):
        return pl.ds(pl.multiple_of(i * CHUNK, CHUNK), CHUNK)

    def outer_forward(load):
        def one(i, carry):
            rows = rows_at(i)
            out = padded_bins([load(n, rows).astype(F32) for n in range(blocks)])
            low = pl.ds(pl.multiple_of(TILE + i * CHUNK, CHUNK), CHUNK)
            for k in range(bins):
                re, im = out[k]
                outer[k, rows, :] = re.astype(BF16)
                outer[k, low, :] = (jnp.zeros_like(re) if im is None else im).astype(BF16)
            return carry

        lax.fori_loop(0, TILE // CHUNK, one, 0)

    def apply(table, k, value):
        both = jnp.dot(table[k], value, preferred_element_type=F32)
        return both[: 2 * TILE] + both[2 * TILE :]

    def times(a, b, conjugate):
        ar, ai = a[:TILE], a[TILE:]
        br, bi = b[:TILE], b[TILE:]
        if conjugate:
            return jnp.concatenate([ar * br + ai * bi, ai * br - ar * bi], 0).astype(BF16)
        return jnp.concatenate([ar * br - ai * bi, ar * bi + ai * br], 0).astype(BF16)

    def outer_back(store):
        def one(i, carry):
            rows = rows_at(i)
            low = pl.ds(pl.multiple_of(TILE + i * CHUNK, CHUNK), CHUNK)
            got = {k: (back[k, rows, :], back[k, low, :]) for k in range(bins)}
            for n, y in enumerate(padded_back(got, blocks)):
                store(n, rows, y)
            return carry

        lax.fori_loop(0, TILE // CHUNK, one, 0)

    def store_send(phase):
        def store(n, rows, y):
            send[phase, n, rows, :] = y.astype(BF16)

        return store

    def store_wide(n, rows, y):
        wide[n, rows, :] = y

    gate(0, k_ref, v_ref)
    pl.semaphore_wait(barrier, blocks - 1 + n_tp - 1)
    start_all(0)
    gate(1, og_ref, q_ref)
    start_all(1)

    for n in range(blocks):
        wide[n] = filt_ref[:, n * TILE : (n + 1) * TILE].T
    outer_forward(lambda n, rows: wide[n, rows, :])
    get_fwd.wait()
    get_inv.wait()

    def filter_step(k, carry):
        spec_f[k] = apply(fwd, k, outer[k])
        return carry

    lax.fori_loop(0, bins, filter_step, 0)

    arrive_all(0)
    outer_forward(lambda n, rows: recv[0, n, rows, :])

    def gated_step(k, carry):
        spec = apply(fwd, k, outer[k])
        spec_kv[k] = spec
        back[k] = apply(inv, k, times(spec, spec_f[k], False))
        return carry

    lax.fori_loop(0, bins, gated_step, 0)
    outer_back(store_send(2))
    recv[2, me] = send[2, me]
    start_all(2)

    arrive_all(1)
    outer_forward(lambda n, rows: recv[1, n, rows, :])

    def gate_step(k, carry):
        spec = apply(fwd, k, outer[k])
        spec_gg[k] = spec
        back[k] = apply(inv, k, times(spec, spec_f[k], True))
        return carry

    lax.fori_loop(0, bins, gate_step, 0)
    outer_back(store_send(3))
    recv[3, me] = send[3, me]
    start_all(3)

    def raw_step(k, carry):
        back[k] = apply(inv, k, times(spec_gg[k], spec_kv[k], True))
        return carry

    lax.fori_loop(0, bins, raw_step, 0)
    outer_back(store_wide)
    total = jnp.zeros((8, TILE), F32)
    for n in range(blocks):
        tile = wide[n]
        raw_ref[:, n * TILE : (n + 1) * TILE] = tile.T
        total = total + jnp.sum((tile * tile).reshape(TILE // 8, 8, TILE), 0)
    sq_mine[...] = total

    def tp_copy(j):
        return pltpu.make_async_remote_copy(
            src_ref=sq_mine,
            dst_ref=sq_tp.at[j - 1],
            send_sem=tp_send.at[j - 1],
            recv_sem=tp_recv.at[j - 1],
            device_id={"tp": lax.rem(my_tp + j, n_tp)},
            device_id_type=MESH,
        )

    for j in range(1, n_tp):
        tp_copy(j).start()
    for j in range(1, n_tp):
        tp_copy(j).wait()
        total = total + sq_tp[j - 1]
    sq_pair[...] = total
    sq_all[me] = total

    def sq_out(d):
        return pltpu.make_async_remote_copy(
            src_ref=sq_pair,
            dst_ref=sq_all.at[me],
            send_sem=sq_send.at[d],
            recv_sem=sq_recv.at[me],
            device_id=place(d),
            device_id_type=MESH,
        )

    def sq_in(s):
        return pltpu.make_async_remote_copy(
            src_ref=sq_pair,
            dst_ref=sq_all.at[s],
            send_sem=sq_send.at[s],
            recv_sem=sq_recv.at[s],
            device_id=place(s),
            device_id_type=MESH,
        )

    def sq_start(j, carry):
        sq_out(lax.rem(me + j, blocks)).start()
        return carry

    def sq_arrive(j, carry):
        sq_in(lax.rem(me + blocks - j, blocks)).wait_recv()
        return carry

    lax.fori_loop(1, blocks, sq_start, 0)

    arrive_all(2)
    for s in range(blocks):
        co_ref[:, s * TILE : (s + 1) * TILE] = recv[2, s]
    lax.fori_loop(1, blocks, sq_arrive, 0)
    mean = jnp.sum(jnp.sum(sq_all[...], 0), keepdims=True) / entries
    rms = jnp.sqrt(mean + 1e-06)
    fac_ref[...] = jnp.broadcast_to(jnp.minimum(1.0, 1.0 / rms), (8, TILE))
    arrive_all(3)
    for s in range(blocks):
        cg_ref[:, s * TILE : (s + 1) * TILE] = recv[3, s]

    def sent(j, carry):
        d = lax.rem(me + j, blocks)
        for phase in range(4):
            out_copy(phase, d).wait_send()
        sq_out(d).wait_send()
        return carry

    lax.fori_loop(1, blocks, sent, 0)


def fused_body(mesh, query_proj, key_proj, value_proj, output_grad, long_filter):
    n_blk, n_ctx, n_tp = mesh.shape["blk"], mesh.shape["ctx"], mesh.shape["tp"]
    blocks = n_blk * n_ctx
    bins = blocks + 1
    tokens, width = query_proj.shape
    chan_count, seq_length = long_filter.shape[1:]
    entries = float(chan_count * seq_length * blocks * n_tp)
    fwd, inv = inner_tables(blocks)
    vmem = pl.BlockSpec(memory_space=pltpu.VMEM)
    hbm = pl.BlockSpec(memory_space=pl.ANY)
    dma = pltpu.SemaphoreType.DMA
    spec = pltpu.VMEM((bins, 2 * TILE, TILE), F32)
    flops = 6 * bins * 2 * 4 * TILE * 2 * TILE * TILE
    conv_out, conv_grad, filter_raw, factor = pl.pallas_call(
        functools.partial(fused_kernel, (blocks, n_ctx, n_tp, entries)),
        out_shape=(
            jax.ShapeDtypeStruct((tokens, width), BF16),
            jax.ShapeDtypeStruct((tokens, width), BF16),
            jax.ShapeDtypeStruct((chan_count, seq_length), F32),
            jax.ShapeDtypeStruct((8, TILE), F32),
        ),
        in_specs=[vmem] * 5 + [hbm] * 2,
        out_specs=(vmem,) * 4,
        scratch_shapes=[
            pltpu.VMEM(fwd.shape, BF16),
            pltpu.VMEM(inv.shape, BF16),
            pltpu.VMEM((4, blocks, TILE, TILE), BF16),
            pltpu.VMEM((4, blocks, TILE, TILE), BF16),
            pltpu.VMEM((bins, 2 * TILE, TILE), BF16),
            spec, spec, spec, spec,
            pltpu.VMEM((blocks, TILE, TILE), F32),
            pltpu.VMEM((8, TILE), F32),
            pltpu.VMEM((max(n_tp - 1, 1), 8, TILE), F32),
            pltpu.VMEM((8, TILE), F32),
            pltpu.VMEM((blocks, 8, TILE), F32),
            dma((2,)),
            dma((4, blocks)),
            dma((4, blocks)),
            dma((blocks,)),
            dma((blocks,)),
            dma((max(n_tp - 1, 1),)),
            dma((max(n_tp - 1, 1),)),
        ],
        compiler_params=pltpu.CompilerParams(
            collective_id=0, has_side_effects=True, vmem_limit_bytes=50 * 1024 * 1024
        ),
        cost_estimate=pl.CostEstimate(
            flops=flops, bytes_accessed=16 * tokens * width, transcendentals=0
        ),
    )(
        key_proj, value_proj, query_proj, output_grad,
        long_filter.reshape(chan_count, seq_length),
        jnp.asarray(fwd), jnp.asarray(inv),
    )
    query_grad = gated_product(output_grad, conv_out)
    key_grad = gated_product(conv_grad, value_proj)
    value_grad = gated_product(conv_grad, key_proj)
    filter_grad = (filter_raw * factor[0, 0]).reshape(1, chan_count, seq_length)
    return (query_grad, key_grad, value_grad, filter_grad)


def general_body(query_proj, key_proj, value_proj, output_grad, long_filter):
    axes = ("blk", "ctx")
    chan_count = long_filter.shape[1]
    seq_length = long_filter.shape[2]
    kernel_cols = long_filter.reshape(chan_count, seq_length)

    def to_channels(rows):
        return lax.all_to_all(rows.T, axes, split_axis=0, concat_axis=1, tiled=True)

    def to_tokens(cols):
        return lax.all_to_all(cols, axes, split_axis=1, concat_axis=0, tiled=True).T

    gated_cols = to_channels(gated_product(key_proj, value_proj))
    gate_cols = to_channels(gated_product(output_grad, query_proj))
    conv_out, conv_grad, filter_raw = channel_work(gated_cols, gate_cols, kernel_cols)
    conv_out, conv_grad = to_tokens(conv_out), to_tokens(conv_grad)
    query_grad = gated_product(output_grad, conv_out)
    key_grad = gated_product(conv_grad, value_proj)
    value_grad = gated_product(conv_grad, key_proj)
    square_total = lax.psum(jnp.sum(filter_raw * filter_raw), ("blk", "ctx", "tp"))
    entry_count = (
        chan_count * seq_length * lax.axis_size("blk") * lax.axis_size("ctx") * lax.axis_size("tp")
    )
    grad_rms = jnp.sqrt(square_total / entry_count + 1e-06)
    factor = jnp.minimum(1.0, 1.0 / grad_rms)
    filter_grad = (filter_raw * factor).reshape(1, chan_count, seq_length)
    return (query_grad, key_grad, value_grad, filter_grad)


def body(mesh, *args):
    blocks = mesh.shape["blk"] * mesh.shape["ctx"]
    fits = args[0].shape[0] == TILE and args[4].shape[1] == TILE and blocks in (4, 8, 16)
    if fits:
        return fused_body(mesh, *args)
    return general_body(*args)


def solution(mesh):
    in_specs = (
        P(("blk", "ctx"), "tp"),
        P(("blk", "ctx"), "tp"),
        P(("blk", "ctx"), "tp"),
        P(("blk", "ctx"), "tp"),
        P("tp", ("blk", "ctx"), None),
    )
    out_specs = (
        P(("blk", "ctx"), "tp"),
        P(("blk", "ctx"), "tp"),
        P(("blk", "ctx"), "tp"),
        P("tp", ("blk", "ctx"), None),
    )
    return jax.shard_map(
        functools.partial(body, mesh), mesh=mesh, in_specs=in_specs, out_specs=out_specs, check_vma=False
    )
```

profile of v0, /device:TPU:0, one launch (start us, length us, event | category | flops | bytes accessed | tf_op | source)
XLA Modules:
  0.0 69.6 jit_solution(13917990054575289446)
XLA Ops:
  0.6 0.0 copy-start
  0.6 1.0 %copy-done = bf16[128,2048]{1,0:T(8,128)(2,1)S(1)} copy-done((bf16[128,2048]{1,0:T(8,128)(2,1)S(1)}, bf16[128,2048]{1,0:T(8,128)(2,1)}, u32[]{:S(2)}) %copy-start) | copy-done | bytes 524312
  1.7 0.0 copy-start.1
  1.7 1.0 %copy-done.1 = bf16[128,2048]{1,0:T(8,128)(2,1)S(1)} copy-done((bf16[128,2048]{1,0:T(8,128)(2,1)S(1)}, bf16[128,2048]{1,0:T(8,128)(2,1)}, u32[]{:S(2)}) %copy-start.1) | copy-done | bytes 524312
  2.7 0.0 copy-start.2
  2.7 1.0 %copy-done.2 = bf16[128,2048]{1,0:T(8,128)(2,1)S(1)} copy-done((bf16[128,2048]{1,0:T(8,128)(2,1)S(1)}, bf16[128,2048]{1,0:T(8,128)(2,1)}, u32[]{:S(2)}) %copy-start.2) | copy-done | bytes 524312
  3.8 0.0 copy-start.3
  3.8 1.0 %copy-done.3 = bf16[128,2048]{1,0:T(8,128)(2,1)S(1)} copy-done((bf16[128,2048]{1,0:T(8,128)(2,1)S(1)}, bf16[128,2048]{1,0:T(8,128)(2,1)}, u32[]{:S(2)}) %copy-start.3) | copy-done | bytes 524312
  4.8 61.0 %shard_map.102 = (bf16[128,2048]{1,0:T(8,128)(2,1)S(1)}, bf16[128,2048]{1,0:T(8,128)(2,1)S(1)}, f32[128,2048]{1,0:T(8,128)}, f32[8,128]{1,0:T(8,128)S(1)}) custom-call(bf16[128,2048]{1,0:T(8,128)(2,1)S(1)} %copy-done, bf16[128,2048]{1,0:T(8,128)(2,1)S(1)} %copy-done.1, bf16[128,2048]{1,0:T(8,128)(2,1)S(1)} %copy-done.3, bf16[128,2048]{1,0:T(8,128)(2,1)S(1)} %copy-done.2, ...), custom_call_target="tpu_custom_call" | custom-call | flops 3422552064 | bytes 4194304 | tf_op jit(solution)/shard_map/pallas_call | solution.py:499
  65.8 0.0 copy-start.4
  65.8 0.5 slice.3
  66.3 1.5 %fusion.1 = (bf16[128,2048]{1,0:T(8,128)(2,1)}, bf16[128,2048]{1,0:T(8,128)(2,1)}, bf16[128,2048]{1,0:T(8,128)(2,1)}) fusion(bf16[128,2048]{1,0:T(8,128)(2,1)S(1)} %get-tuple-element.9, bf16[128,2048]{1,0:T(8,128)(2,1)S(1)} %copy-done, bf16[128,2048]{1,0:T(8,128)(2,1)S(1)} %copy-done.1, bf16[128,2048]{1,0:T(8,128)(2,1)S(1)} %get-tuple-element.8, ...), kind=kLoop, calls=%fused_computation.3 | loop fusion | flops 2883584 | bytes 4194304 | tf_op jit(solution)/shard_map/convert_element_type | solution.py:112
  67.9 0.0 copy-done.4
  67.9 1.7 %multiply_bitcast_fusion = f32[1,128,2048]{2,1,0:T(8,128)} fusion(f32[128,2048]{1,0:T(8,128)S(1)} %copy-done.4, f32[]{:T(128)} %bitcast.1), kind=kLoop, calls=%fused_computation.4 | loop fusion | flops 262144 | bytes 2097156 | tf_op jit(solution)/shard_map/reshape | solution.py:543
Async XLA Ops:
  0.6 1.0 %copy-start = (bf16[128,2048]{1,0:T(8,128)(2,1)S(1)}, bf16[128,2048]{1,0:T(8,128)(2,1)}, u32[]{:S(2)}) copy-start(bf16[128,2048]{1,0:T(8,128)(2,1)} %k_ref.1) | copy-start | bytes 1572868
  1.7 1.0 %copy-start.1 = (bf16[128,2048]{1,0:T(8,128)(2,1)S(1)}, bf16[128,2048]{1,0:T(8,128)(2,1)}, u32[]{:S(2)}) copy-start(bf16[128,2048]{1,0:T(8,128)(2,1)} %v_ref.1) | copy-start | bytes 1572868
  2.7 1.0 %copy-start.2 = (bf16[128,2048]{1,0:T(8,128)(2,1)S(1)}, bf16[128,2048]{1,0:T(8,128)(2,1)}, u32[]{:S(2)}) copy-start(bf16[128,2048]{1,0:T(8,128)(2,1)} %og_ref.1) | copy-start | bytes 1572868
  3.8 1.0 %copy-start.3 = (bf16[128,2048]{1,0:T(8,128)(2,1)S(1)}, bf16[128,2048]{1,0:T(8,128)(2,1)}, u32[]{:S(2)}) copy-start(bf16[128,2048]{1,0:T(8,128)(2,1)} %q_ref.1) | copy-start | bytes 1572868
  65.8 2.1 %copy-start.4 = (f32[128,2048]{1,0:T(8,128)S(1)}, f32[128,2048]{1,0:T(8,128)}, u32[]{:S(2)}) copy-start(f32[128,2048]{1,0:T(8,128)} %get-tuple-element.10) | copy-start | bytes 3145732
where the time goes:
time: 70.7 us; the launch traced here: 69.6 us
  Pallas kernels  61 us (86%)
  local copies, waits for them, and re-layouts  4.7 us (7%)
  other arithmetic  3.21 us (5%)
    pallas_call x1, Pallas kernels, fused_body(): pl.pallas_call(functools.partial(fused_kernel, (blocks, n_ctx, n_tp, entr...  61 us
    unnamed x10, local copies, waits for them, and re-layouts  4.16 us
    reshape x1, other arithmetic, fused_body(): filter_grad = (filter_raw * factor[0, 0]).reshape(1, chan_count, seq_length)  1.69 us
    convert_element_type x1, other arithmetic, gated_product(): (left.astype(jnp.float32) * right.astype(jnp.float32)).astype(jnp.bfloat16)  1.52 us

commit v1 on v0

--- a/solution.py
+++ b/solution.py
@@ -14,6 +14,7 @@
 MESH = pl.DeviceIdType.MESH
 TILE = 128
 CHUNK = 16
+GROUP = 2
 F32 = jnp.float32
 BF16 = jnp.bfloat16
 
@@ -226,21 +227,16 @@
     weight = np.where((k1 == 0) | (k1 == blocks), 1.0, 2.0) / full
     inv = fwd.transpose(0, 2, 1) * weight
 
-    def parts(m):
-        hi = m.astype(ml_dtypes.bfloat16)
-        lo = (m - hi.astype(np.float64)).astype(ml_dtypes.bfloat16)
-        return np.concatenate([hi, lo], 1)
-
-    return parts(fwd), parts(inv)
+    return fwd.astype(ml_dtypes.bfloat16), inv.astype(ml_dtypes.bfloat16)
 
 
 def fused_kernel(
     cfg,
-    k_ref, v_ref, q_ref, og_ref, filt_ref, fwd_hbm, inv_hbm,
-    co_ref, cg_ref, raw_ref, fac_ref,
-    fwd, inv, send, recv, outer, spec_f, spec_kv, spec_gg, back, wide,
+    k_hbm, v_hbm, q_hbm, og_hbm, filt_hbm, fwd_hbm, inv_hbm,
+    co_hbm, cg_hbm, raw_hbm, fac_ref,
+    k_ref, v_ref, q_ref, og_ref, filt_ref, raw_ref, fwd, inv, send, recv, outer, spec_f, spec_kv, spec_gg, back, wide,
     sq_mine, sq_tp, sq_pair, sq_all,
-    table_sem, send_sem, recv_sem, sq_send, sq_recv, tp_send, tp_recv,
+    load_sem, store_sem, raw_sem, table_sem, send_sem, recv_sem, sq_send, sq_recv, tp_send, tp_recv,
 ):
     blocks, n_ctx, n_tp, entries = cfg
     me = lax.axis_index("blk") * n_ctx + lax.axis_index("ctx")
@@ -250,6 +246,21 @@
     def place(d):
         return {"blk": d // n_ctx, "ctx": d % n_ctx}
 
+    quarter = k_ref.shape[1] // 4
+
+    def load(which, part):
+        hbm, vmem = (
+            (k_hbm, k_ref), (v_hbm, v_ref), (og_hbm, og_ref), (q_hbm, q_ref), (filt_hbm, filt_ref)
+        )[which]
+        cols = pl.ds(part * quarter, quarter)
+        return pltpu.make_async_copy(
+            hbm.at[:, cols], vmem.at[:, cols], load_sem.at[which, part]
+        )
+
+    for pair in ((0, 1), (2, 3), (4,)):
+        for part in range(4):
+            for which in pair:
+                load(which, part).start()
     get_fwd = pltpu.make_async_copy(fwd_hbm, fwd, table_sem.at[0])
     get_inv = pltpu.make_async_copy(inv_hbm, inv, table_sem.at[1])
     get_fwd.start()
@@ -270,6 +281,9 @@
 
     def gate(phase, a_ref, b_ref):
         for d in range(blocks):
+            if d % (blocks // 4) == 0:
+                load(2 * phase, d // (blocks // 4)).wait()
+                load(2 * phase + 1, d // (blocks // 4)).wait()
             cols = slice(d * TILE, (d + 1) * TILE)
             send[phase, d] = gated_product(a_ref[:, cols], b_ref[:, cols])
         recv[phase, me] = send[phase, me]
@@ -294,12 +308,24 @@
             device_id_type=MESH,
         )
 
+    def flipped(place_on_axis, mask):
+        out, weight = 0, 1
+        while weight < n_ctx:
+            bit = lax.rem(place_on_axis // weight, 2)
+            out = out + weight * (1 - bit if mask & weight else bit)
+            weight *= 2
+        return out
+
     def start_all(phase):
-        def one(j, carry):
-            out_copy(phase, lax.rem(me + j, blocks)).start()
-            return carry
-
-        lax.fori_loop(1, blocks, one, 0)
+        for mask in range(n_ctx - 1, -1, -1):
+            ctx = flipped(lax.axis_index("ctx"), mask)
+
+            def one(j, carry, ctx=ctx):
+                blk = lax.rem(lax.axis_index("blk") + j, blocks // n_ctx)
+                out_copy(phase, blk * n_ctx + ctx).start()
+                return carry
+
+            lax.fori_loop(0 if mask else 1, blocks // n_ctx, one, 0)
 
     def arrive_all(phase):
         def one(j, carry):
@@ -325,8 +351,7 @@
         lax.fori_loop(0, TILE // CHUNK, one, 0)
 
     def apply(table, k, value):
-        both = jnp.dot(table[k], value, preferred_element_type=F32)
-        return both[: 2 * TILE] + both[2 * TILE :]
+        return jnp.dot(table[k], value, preferred_element_type=F32)
 
     def times(a, b, conjugate):
         ar, ai = a[:TILE], a[TILE:]
@@ -361,28 +386,42 @@
     gate(1, og_ref, q_ref)
     start_all(1)
 
+    for part in range(4):
+        load(4, part).wait()
     for n in range(blocks):
         wide[n] = filt_ref[:, n * TILE : (n + 1) * TILE].T
     outer_forward(lambda n, rows: wide[n, rows, :])
     get_fwd.wait()
     get_inv.wait()
 
-    def filter_step(k, carry):
-        spec_f[k] = apply(fwd, k, outer[k])
-        return carry
-
-    lax.fori_loop(0, bins, filter_step, 0)
+    def each_bin(step):
+        def group(i, carry):
+            step([GROUP * i + g for g in range(GROUP)])
+            return carry
+
+        lax.fori_loop(0, bins // GROUP, group, 0)
+        if bins % GROUP:
+            step(list(range(bins - bins % GROUP, bins)))
+
+    def filter_step(ks):
+        specs = [apply(fwd, k, outer[k]) for k in ks]
+        for k, spec in zip(ks, specs):
+            spec_f[k] = spec
+
+    each_bin(filter_step)
 
     arrive_all(0)
     outer_forward(lambda n, rows: recv[0, n, rows, :])
 
-    def gated_step(k, carry):
-        spec = apply(fwd, k, outer[k])
-        spec_kv[k] = spec
-        back[k] = apply(inv, k, times(spec, spec_f[k], False))
-        return carry
-
-    lax.fori_loop(0, bins, gated_step, 0)
+    def gated_step(ks):
+        specs = [apply(fwd, k, outer[k]) for k in ks]
+        products = [times(spec, spec_f[k], False) for k, spec in zip(ks, specs)]
+        results = [apply(inv, k, product) for k, product in zip(ks, products)]
+        for k, spec, result in zip(ks, specs, results):
+            spec_kv[k] = spec
+            back[k] = result
+
+    each_bin(gated_step)
     outer_back(store_send(2))
     recv[2, me] = send[2, me]
     start_all(2)
@@ -390,28 +429,34 @@
     arrive_all(1)
     outer_forward(lambda n, rows: recv[1, n, rows, :])
 
-    def gate_step(k, carry):
-        spec = apply(fwd, k, outer[k])
-        spec_gg[k] = spec
-        back[k] = apply(inv, k, times(spec, spec_f[k], True))
-        return carry
-
-    lax.fori_loop(0, bins, gate_step, 0)
+    def gate_step(ks):
+        specs = [apply(fwd, k, outer[k]) for k in ks]
+        products = [times(spec, spec_f[k], True) for k, spec in zip(ks, specs)]
+        results = [apply(inv, k, product) for k, product in zip(ks, products)]
+        for k, spec, result in zip(ks, specs, results):
+            spec_gg[k] = spec
+            back[k] = result
+
+    each_bin(gate_step)
     outer_back(store_send(3))
     recv[3, me] = send[3, me]
     start_all(3)
 
-    def raw_step(k, carry):
-        back[k] = apply(inv, k, times(spec_gg[k], spec_kv[k], True))
-        return carry
-
-    lax.fori_loop(0, bins, raw_step, 0)
+    def raw_step(ks):
+        products = [times(spec_gg[k], spec_kv[k], True) for k in ks]
+        results = [apply(inv, k, product) for k, product in zip(ks, products)]
+        for k, result in zip(ks, results):
+            back[k] = result
+
+    each_bin(raw_step)
     outer_back(store_wide)
     total = jnp.zeros((8, TILE), F32)
     for n in range(blocks):
         tile = wide[n]
         raw_ref[:, n * TILE : (n + 1) * TILE] = tile.T
         total = total + jnp.sum((tile * tile).reshape(TILE // 8, 8, TILE), 0)
+    put_raw = pltpu.make_async_copy(raw_ref, raw_hbm, raw_sem)
+    put_raw.start()
     sq_mine[...] = total
 
     def tp_copy(j):
@@ -462,16 +507,35 @@
 
     lax.fori_loop(1, blocks, sq_start, 0)
 
-    arrive_all(2)
-    for s in range(blocks):
-        co_ref[:, s * TILE : (s + 1) * TILE] = recv[2, s]
+    def put(phase, hbm, s):
+        return pltpu.make_async_copy(
+            recv.at[phase, s],
+            hbm.at[:, pl.ds(pl.multiple_of(s * TILE, TILE), TILE)],
+            store_sem.at[phase - 2, s],
+        )
+
+    def put_all(phase, hbm):
+        put(phase, hbm, me).start()
+
+        def one(j, carry):
+            s = lax.rem(me + blocks - j, blocks)
+            in_copy(phase, s).wait_recv()
+            put(phase, hbm, s).start()
+            return carry
+
+        lax.fori_loop(1, blocks, one, 0)
+
+    put_all(2, co_hbm)
     lax.fori_loop(1, blocks, sq_arrive, 0)
     mean = jnp.sum(jnp.sum(sq_all[...], 0), keepdims=True) / entries
     rms = jnp.sqrt(mean + 1e-06)
-    fac_ref[...] = jnp.broadcast_to(jnp.minimum(1.0, 1.0 / rms), (8, TILE))
-    arrive_all(3)
-    for s in range(blocks):
-        cg_ref[:, s * TILE : (s + 1) * TILE] = recv[3, s]
+    fac_ref[...] = jnp.minimum(1.0, 1.0 / rms)
+    put_all(3, cg_hbm)
+
+    def stored(s, carry):
+        put(2, co_hbm, s).wait()
+        put(3, cg_hbm, s).wait()
+        return carry
 
     def sent(j, carry):
         d = lax.rem(me + j, blocks)
@@ -481,6 +545,8 @@
         return carry
 
     lax.fori_loop(1, blocks, sent, 0)
+    put_raw.wait()
+    lax.fori_loop(0, blocks, stored, 0)
 
 
 def fused_body(mesh, query_proj, key_proj, value_proj, output_grad, long_filter):
@@ -492,21 +558,24 @@
     entries = float(chan_count * seq_length * blocks * n_tp)
     fwd, inv = inner_tables(blocks)
     vmem = pl.BlockSpec(memory_space=pltpu.VMEM)
-    hbm = pl.BlockSpec(memory_space=pl.ANY)
+    hbm = pl.BlockSpec(memory_space=pltpu.HBM)
+    stream = pltpu.VMEM((tokens, width), BF16)
+    lags = pltpu.VMEM((chan_count, seq_length), F32)
     dma = pltpu.SemaphoreType.DMA
     spec = pltpu.VMEM((bins, 2 * TILE, TILE), F32)
-    flops = 6 * bins * 2 * 4 * TILE * 2 * TILE * TILE
+    flops = 6 * bins * 2 * 2 * TILE * 2 * TILE * TILE
     conv_out, conv_grad, filter_raw, factor = pl.pallas_call(
         functools.partial(fused_kernel, (blocks, n_ctx, n_tp, entries)),
         out_shape=(
             jax.ShapeDtypeStruct((tokens, width), BF16),
             jax.ShapeDtypeStruct((tokens, width), BF16),
             jax.ShapeDtypeStruct((chan_count, seq_length), F32),
-            jax.ShapeDtypeStruct((8, TILE), F32),
+            jax.ShapeDtypeStruct((1, 1), F32),
         ),
-        in_specs=[vmem] * 5 + [hbm] * 2,
-        out_specs=(vmem,) * 4,
+        in_specs=[hbm] * 7,
+        out_specs=(hbm, hbm, hbm, vmem),
         scratch_shapes=[
+            stream, stream, stream, stream, lags, lags,
             pltpu.VMEM(fwd.shape, BF16),
             pltpu.VMEM(inv.shape, BF16),
             pltpu.VMEM((4, blocks, TILE, TILE), BF16),
@@ -518,6 +587,9 @@
             pltpu.VMEM((max(n_tp - 1, 1), 8, TILE), F32),
             pltpu.VMEM((8, TILE), F32),
             pltpu.VMEM((blocks, 8, TILE), F32),
+            dma((5, 4)),
+            dma((2, blocks)),
+            dma(()),
             dma((2,)),
             dma((4, blocks)),
             dma((4, blocks)),
@@ -540,7 +612,7 @@
     query_grad = gated_product(output_grad, conv_out)
     key_grad = gated_product(conv_grad, value_proj)
     value_grad = gated_product(conv_grad, key_proj)
-    filter_grad = (filter_raw * factor[0, 0]).reshape(1, chan_count, seq_length)
+    filter_grad = (filter_raw * factor.reshape(())).reshape(1, chan_count, seq_length)
     return (query_grad, key_grad, value_grad, filter_grad)
 
 

time: 70.7 us -> 66.2 us (0.936); the launches traced: 69.6 us -> 65.9 us
  Pallas kernels: 61 us -> 57.8 us
    pallas_call x1, Pallas kernels: 61 us -> 57.8 us  [fused_body(): pl.pallas_call(functools.partial(fused_kernel, (blocks, n_ctx, n_tp, entr...]
where the time goes in v1:
time: 66.2 us; the launch traced here: 65.9 us
  Pallas kernels  57.8 us (87%)
  local copies, waits for them, and re-layouts  4.16 us (6%)
  other arithmetic  3.22 us (5%)
    pallas_call x1, Pallas kernels, fused_body(): pl.pallas_call(functools.partial(fused_kernel, (blocks, n_ctx, n_tp, entr...  57.8 us
    unnamed x10, local copies, waits for them, and re-layouts  4.16 us
    reshape x1, other arithmetic, fused_body(): (filter_raw * factor.reshape(())).reshape(1, chan_count, seq_length)  1.69 us
    convert_element_type x1, other arithmetic, gated_product(): (left.astype(jnp.float32) * right.astype(jnp.float32)).astype(jnp.bfloat16)  1.52 us

profile of v1, /device:TPU:0, one launch (start us, length us, event | category | flops | bytes accessed | tf_op | source)
XLA Modules:
  0.0 65.9 jit_solution(9189044334701041432)
XLA Ops:
  0.6 0.0 copy-start
  0.6 1.0 %copy-done = bf16[128,2048]{1,0:T(8,128)(2,1)S(1)} copy-done((bf16[128,2048]{1,0:T(8,128)(2,1)S(1)}, bf16[128,2048]{1,0:T(8,128)(2,1)}, u32[]{:S(2)}) %copy-start) | copy-done | bytes 524312
  1.7 0.0 copy-start.1
  1.7 1.0 %copy-done.1 = bf16[128,2048]{1,0:T(8,128)(2,1)S(1)} copy-done((bf16[128,2048]{1,0:T(8,128)(2,1)S(1)}, bf16[128,2048]{1,0:T(8,128)(2,1)}, u32[]{:S(2)}) %copy-start.1) | copy-done | bytes 524312
  2.7 0.0 copy-start.2
  2.7 1.0 %copy-done.2 = bf16[128,2048]{1,0:T(8,128)(2,1)S(1)} copy-done((bf16[128,2048]{1,0:T(8,128)(2,1)S(1)}, bf16[128,2048]{1,0:T(8,128)(2,1)}, u32[]{:S(2)}) %copy-start.2) | copy-done | bytes 524312
  3.8 0.0 copy-start.3
  3.8 1.0 %copy-done.3 = bf16[128,2048]{1,0:T(8,128)(2,1)S(1)} copy-done((bf16[128,2048]{1,0:T(8,128)(2,1)S(1)}, bf16[128,2048]{1,0:T(8,128)(2,1)}, u32[]{:S(2)}) %copy-start.3) | copy-done | bytes 524312
  4.8 57.8 %shard_map.102 = (bf16[128,2048]{1,0:T(8,128)(2,1)S(1)}, bf16[128,2048]{1,0:T(8,128)(2,1)S(1)}, f32[128,2048]{1,0:T(8,128)}, f32[1,1]{1,0:T(1,128)}) custom-call(bf16[128,2048]{1,0:T(8,128)(2,1)S(1)} %copy-done, bf16[128,2048]{1,0:T(8,128)(2,1)S(1)} %copy-done.1, bf16[128,2048]{1,0:T(8,128)(2,1)S(1)} %copy-done.3, bf16[128,2048]{1,0:T(8,128)(2,1)S(1)} %copy-done.2, ...), custom_call_target="tpu_custom_call" | custom-call | flops 1711276032 | bytes 4194304 | tf_op jit(solution)/shard_map/pallas_call | solution.py:567
  62.6 0.0 copy-start.4
  62.6 1.5 %fusion.1 = (bf16[128,2048]{1,0:T(8,128)(2,1)}, bf16[128,2048]{1,0:T(8,128)(2,1)}, bf16[128,2048]{1,0:T(8,128)(2,1)}) fusion(bf16[128,2048]{1,0:T(8,128)(2,1)S(1)} %get-tuple-element.9, bf16[128,2048]{1,0:T(8,128)(2,1)S(1)} %copy-done, bf16[128,2048]{1,0:T(8,128)(2,1)S(1)} %copy-done.1, bf16[128,2048]{1,0:T(8,128)(2,1)S(1)} %get-tuple-element.8, ...), kind=kLoop, calls=%fused_computation.3 | loop fusion | flops 2883584 | bytes 4194304 | tf_op jit(solution)/shard_map/convert_element_type | solution.py:113
  64.2 0.0 copy-done.4
  64.2 1.7 %multiply_bitcast_fusion = f32[1,128,2048]{2,1,0:T(8,128)} fusion(f32[128,2048]{1,0:T(8,128)S(1)} %copy-done.4, f32[]{:T(128)} %bitcast.1), kind=kLoop, calls=%fused_computation.4 | loop fusion | flops 262144 | bytes 2097156 | tf_op jit(solution)/shard_map/reshape | solution.py:615
Async XLA Ops:
  0.6 1.0 %copy-start = (bf16[128,2048]{1,0:T(8,128)(2,1)S(1)}, bf16[128,2048]{1,0:T(8,128)(2,1)}, u32[]{:S(2)}) copy-start(bf16[128,2048]{1,0:T(8,128)(2,1)} %k_hbm.1) | copy-start | bytes 1572868
  1.7 1.0 %copy-start.1 = (bf16[128,2048]{1,0:T(8,128)(2,1)S(1)}, bf16[128,2048]{1,0:T(8,128)(2,1)}, u32[]{:S(2)}) copy-start(bf16[128,2048]{1,0:T(8,128)(2,1)} %v_hbm.1) | copy-start | bytes 1572868
  2.7 1.0 %copy-start.2 = (bf16[128,2048]{1,0:T(8,128)(2,1)S(1)}, bf16[128,2048]{1,0:T(8,128)(2,1)}, u32[]{:S(2)}) copy-start(bf16[128,2048]{1,0:T(8,128)(2,1)} %og_hbm.1) | copy-start | bytes 1572868
  3.8 1.0 %copy-start.3 = (bf16[128,2048]{1,0:T(8,128)(2,1)S(1)}, bf16[128,2048]{1,0:T(8,128)(2,1)}, u32[]{:S(2)}) copy-start(bf16[128,2048]{1,0:T(8,128)(2,1)} %q_hbm.1) | copy-start | bytes 1572868
  62.6 1.5 %copy-start.4 = (f32[128,2048]{1,0:T(8,128)S(1)}, f32[128,2048]{1,0:T(8,128)}, u32[]{:S(2)}) copy-start(f32[128,2048]{1,0:T(8,128)} %get-tuple-element.10) | copy-start | bytes 3145732

commit v2 on v1

--- a/solution.py
+++ b/solution.py
@@ -13,8 +13,10 @@
 PRECISE = lax.Precision.HIGH
 MESH = pl.DeviceIdType.MESH
 TILE = 128
+PARTS = 4
 CHUNK = 16
-GROUP = 2
+GROUP = 4
+VMEM_LIMIT = 63 * 1024 * 1024
 F32 = jnp.float32
 BF16 = jnp.bfloat16
 
@@ -547,6 +549,41 @@
     lax.fori_loop(1, blocks, sent, 0)
     put_raw.wait()
     lax.fori_loop(0, blocks, stored, 0)
+
+
+def finish_kernel(
+    og_hbm, v_hbm, k_hbm, co_hbm, cg_hbm, raw_hbm, fac_ref,
+    qg_hbm, kg_hbm, vg_hbm, fg_hbm,
+    og, v, k, co, cg, raw, qg, kg, vg, fg, load_sem, store_sem,
+):
+    loads = ((og_hbm, og), (co_hbm, co), (cg_hbm, cg), (v_hbm, v), (k_hbm, k), (raw_hbm, raw))
+    stores = ((qg, qg_hbm), (kg, kg_hbm), (vg, vg_hbm), (fg, fg_hbm))
+    step = og.shape[0] // PARTS
+
+    def copies(pairs, sems, part):
+        rows = pl.ds(part * step, step)
+        return [
+            pltpu.make_async_copy(src.at[rows], dst.at[rows], sems.at[i, part])
+            for i, (src, dst) in enumerate(pairs)
+        ]
+
+    for part in range(PARTS):
+        for copy in copies(loads, load_sem, part):
+            copy.start()
+    for part in range(PARTS):
+        for copy in copies(loads, load_sem, part):
+            copy.wait()
+        rows = slice(part * step, (part + 1) * step)
+        qg[rows] = gated_product(og[rows], co[rows])
+        grad = cg[rows]
+        kg[rows] = gated_product(grad, v[rows])
+        vg[rows] = gated_product(grad, k[rows])
+        fg[rows] = raw[rows] * fac_ref[...]
+        for copy in copies(stores, store_sem, part):
+            copy.start()
+    for part in range(PARTS):
+        for copy in copies(stores, store_sem, part):
+            copy.wait()
 
 
 def fused_body(mesh, query_proj, key_proj, value_proj, output_grad, long_filter):
@@ -599,7 +636,7 @@
             dma((max(n_tp - 1, 1),)),
         ],
         compiler_params=pltpu.CompilerParams(
-            collective_id=0, has_side_effects=True, vmem_limit_bytes=50 * 1024 * 1024
+            collective_id=0, has_side_effects=True, vmem_limit_bytes=VMEM_LIMIT
         ),
         cost_estimate=pl.CostEstimate(
             flops=flops, bytes_accessed=16 * tokens * width, transcendentals=0
@@ -609,10 +646,19 @@
         long_filter.reshape(chan_count, seq_length),
         jnp.asarray(fwd), jnp.asarray(inv),
     )
-    query_grad = gated_product(output_grad, conv_out)
-    key_grad = gated_product(conv_grad, value_proj)
-    value_grad = gated_product(conv_grad, key_proj)
-    filter_grad = (filter_raw * factor.reshape(())).reshape(1, chan_count, seq_length)
+    rows_like = jax.ShapeDtypeStruct((tokens, width), BF16)
+    query_grad, key_grad, value_grad, filter_grad = pl.pallas_call(
+        finish_kernel,
+        out_shape=(rows_like,) * 3 + (jax.ShapeDtypeStruct((chan_count, seq_length), F32),),
+        in_specs=[hbm] * 6 + [vmem],
+        out_specs=(hbm,) * 4,
+        scratch_shapes=[stream] * 5 + [lags] + [stream] * 3 + [lags, dma((6, PARTS)), dma((4, PARTS))],
+        compiler_params=pltpu.CompilerParams(vmem_limit_bytes=VMEM_LIMIT),
+        cost_estimate=pl.CostEstimate(
+            flops=4 * tokens * width, bytes_accessed=24 * tokens * width, transcendentals=0
+        ),
+    )(output_grad, value_proj, key_proj, conv_out, conv_grad, filter_raw, factor)
+    filter_grad = filter_grad.reshape(1, chan_count, seq_length)
     return (query_grad, key_grad, value_grad, filter_grad)
 
 

time: 66.2 us -> 62.5 us (0.944)
  local copies, waits for them, and re-layouts: 4.16 us -> 0 us
  Pallas kernels: 57.8 us -> 61.7 us
  other arithmetic: 3.22 us -> 0 us
    unnamed x10 -> x0, local copies, waits for them, and re-layouts: 4.16 us -> none
    pallas_call x0 -> x1, Pallas kernels: none -> 3.93 us  [fused_body(): pl.pallas_call(finish_kernel, out_shape=(rows_like,) * 3 + (jax.ShapeDtyp...]
    reshape x1 -> x0, other arithmetic: 1.69 us -> none  [fused_body(): (filter_raw * factor.reshape(())).reshape(1, chan_count, seq_length)]
    convert_element_type x1 -> x0, other arithmetic: 1.52 us -> none  [gated_product(): (left.astype(jnp.float32) * right.astype(jnp.float32)).astype(jnp.bfloat16)]
where the time goes in v2:
time: 62.5 us; the launch traced here: 62.3 us
  Pallas kernels  61.7 us (99%)
  between operations  0.64 us (1%)
    pallas_call x1, Pallas kernels, fused_body(): pl.pallas_call(functools.partial(fused_kernel, (blocks, n_ctx, n_tp, entr...  57.7 us
    pallas_call x1, Pallas kernels, fused_body(): pl.pallas_call(finish_kernel, out_shape=(rows_like,) * 3 + (jax.ShapeDtyp...  3.93 us

profile of v2, /device:TPU:0, one launch (start us, length us, event | category | flops | bytes accessed | tf_op | source)
XLA Modules:
  0.0 62.3 jit_solution(15501497316167690101)
XLA Ops:
  0.6 57.7 %shard_map.102 = (bf16[128,2048]{1,0:T(8,128)(2,1)}, bf16[128,2048]{1,0:T(8,128)(2,1)}, f32[128,2048]{1,0:T(8,128)}, f32[1,1]{1,0:T(1,128)}) custom-call(bf16[128,2048]{1,0:T(8,128)(2,1)} %k_hbm.3, bf16[128,2048]{1,0:T(8,128)(2,1)} %v_hbm.3, bf16[128,2048]{1,0:T(8,128)(2,1)} %q_hbm.1, bf16[128,2048]{1,0:T(8,128)(2,1)} %og_hbm.3, f32[128,2048]{1,0:T(8,128)} %bitcast.2, ...), custom_call_target="tpu_custom_call" | custom-call | flops 1711276032 | bytes 4194304 | tf_op jit(solution)/shard_map/pallas_call | solution.py:604
  58.4 3.9 %shard_map.103 = (bf16[128,2048]{1,0:T(8,128)(2,1)}, bf16[128,2048]{1,0:T(8,128)(2,1)}, bf16[128,2048]{1,0:T(8,128)(2,1)}, f32[128,2048]{1,0:T(8,128)}) custom-call(bf16[128,2048]{1,0:T(8,128)(2,1)} %og_hbm.3, bf16[128,2048]{1,0:T(8,128)(2,1)} %v_hbm.3, bf16[128,2048]{1,0:T(8,128)(2,1)} %k_hbm.3, bf16[128,2048]{1,0:T(8,128)(2,1)} %get-tuple-element.12.co_hbm, ...), custom_call_target="tpu_custom_call" | custom-call | flops 1048576 | bytes 6291456 | tf_op jit(solution)/shard_map/pallas_call | solution.py:650

commit v3 on v1

--- a/solution.py
+++ b/solution.py
@@ -13,8 +13,10 @@
 PRECISE = lax.Precision.HIGH
 MESH = pl.DeviceIdType.MESH
 TILE = 128
+PARTS = 4
 CHUNK = 16
-GROUP = 2
+GROUP = 4
+VMEM_LIMIT = 63 * 1024 * 1024
 F32 = jnp.float32
 BF16 = jnp.bfloat16
 
@@ -233,7 +235,7 @@
 def fused_kernel(
     cfg,
     k_hbm, v_hbm, q_hbm, og_hbm, filt_hbm, fwd_hbm, inv_hbm,
-    co_hbm, cg_hbm, raw_hbm, fac_ref,
+    qg_hbm, kg_hbm, vg_hbm, raw_hbm, fac_ref,
     k_ref, v_ref, q_ref, og_ref, filt_ref, raw_ref, fwd, inv, send, recv, outer, spec_f, spec_kv, spec_gg, back, wide,
     sq_mine, sq_tp, sq_pair, sq_all,
     load_sem, store_sem, raw_sem, table_sem, send_sem, recv_sem, sq_send, sq_recv, tp_send, tp_recv,
@@ -316,12 +318,14 @@
             weight *= 2
         return out
 
-    def start_all(phase):
+    def start_all(phase, after=None):
         for mask in range(n_ctx - 1, -1, -1):
             ctx = flipped(lax.axis_index("ctx"), mask)
 
             def one(j, carry, ctx=ctx):
                 blk = lax.rem(lax.axis_index("blk") + j, blocks // n_ctx)
+                if after is not None:
+                    out_copy(after, blk * n_ctx + ctx).wait_send()
                 out_copy(phase, blk * n_ctx + ctx).start()
                 return carry
 
@@ -384,7 +388,6 @@
     pl.semaphore_wait(barrier, blocks - 1 + n_tp - 1)
     start_all(0)
     gate(1, og_ref, q_ref)
-    start_all(1)
 
     for part in range(4):
         load(4, part).wait()
@@ -409,6 +412,7 @@
             spec_f[k] = spec
 
     each_bin(filter_step)
+    start_all(1, after=0)
 
     arrive_all(0)
     outer_forward(lambda n, rows: recv[0, n, rows, :])
@@ -507,39 +511,52 @@
 
     lax.fori_loop(1, blocks, sq_start, 0)
 
-    def put(phase, hbm, s):
+    def columns(s):
+        return pl.ds(pl.multiple_of(s * TILE, TILE), TILE)
+
+    def put(which, s):
+        hbm, slot = ((qg_hbm, 2), (kg_hbm, 3), (vg_hbm, 0))[which]
         return pltpu.make_async_copy(
-            recv.at[phase, s],
-            hbm.at[:, pl.ds(pl.multiple_of(s * TILE, TILE), TILE)],
-            store_sem.at[phase - 2, s],
-        )
-
-    def put_all(phase, hbm):
-        put(phase, hbm, me).start()
+            recv.at[slot, s], hbm.at[:, columns(s)], store_sem.at[which, s]
+        )
+
+    def finish_query(s):
+        recv[2, s] = gated_product(og_ref[:, columns(s)], recv[2, s])
+        put(0, s).start()
+
+    def finish_grad(s):
+        grad = recv[3, s]
+        recv[3, s] = gated_product(grad, v_ref[:, columns(s)])
+        put(1, s).start()
+        recv[0, s] = gated_product(grad, k_ref[:, columns(s)])
+        put(2, s).start()
+
+    def finish_all(phase, finish):
+        finish(me)
 
         def one(j, carry):
             s = lax.rem(me + blocks - j, blocks)
             in_copy(phase, s).wait_recv()
-            put(phase, hbm, s).start()
+            finish(s)
             return carry
 
         lax.fori_loop(1, blocks, one, 0)
 
-    put_all(2, co_hbm)
+    finish_all(2, finish_query)
     lax.fori_loop(1, blocks, sq_arrive, 0)
     mean = jnp.sum(jnp.sum(sq_all[...], 0), keepdims=True) / entries
     rms = jnp.sqrt(mean + 1e-06)
     fac_ref[...] = jnp.minimum(1.0, 1.0 / rms)
-    put_all(3, cg_hbm)
+    finish_all(3, finish_grad)
 
     def stored(s, carry):
-        put(2, co_hbm, s).wait()
-        put(3, cg_hbm, s).wait()
+        for which in range(3):
+            put(which, s).wait()
         return carry
 
     def sent(j, carry):
         d = lax.rem(me + j, blocks)
-        for phase in range(4):
+        for phase in range(1, 4):
             out_copy(phase, d).wait_send()
         sq_out(d).wait_send()
         return carry
@@ -547,6 +564,34 @@
     lax.fori_loop(1, blocks, sent, 0)
     put_raw.wait()
     lax.fori_loop(0, blocks, stored, 0)
+
+
+def finish_kernel(
+    qg_in, kg_in, vg_in, raw_hbm, fac_ref, qg_out, kg_out, vg_out, fg_hbm,
+    raw, fg, move_sem, load_sem, store_sem,
+):
+    step = raw.shape[0] // PARTS
+
+    def copy(src, dst, sem, part):
+        rows = pl.ds(part * step, step)
+        return pltpu.make_async_copy(src.at[rows], dst.at[rows], sem)
+
+    loads = [copy(raw_hbm, raw, load_sem.at[p], p) for p in range(PARTS)]
+    stores = [copy(fg, fg_hbm, store_sem.at[p], p) for p in range(PARTS)]
+    moves = [
+        copy(src, dst, move_sem.at[i, p], p)
+        for p in range(PARTS)
+        for i, (src, dst) in enumerate(((qg_in, qg_out), (kg_in, kg_out), (vg_in, vg_out)))
+    ]
+    for item in loads + moves:
+        item.start()
+    for p in range(PARTS):
+        loads[p].wait()
+        rows = slice(p * step, (p + 1) * step)
+        fg[rows] = raw[rows] * fac_ref[...]
+        stores[p].start()
+    for item in moves + stores:
+        item.wait()
 
 
 def fused_body(mesh, query_proj, key_proj, value_proj, output_grad, long_filter):
@@ -563,17 +608,17 @@
     lags = pltpu.VMEM((chan_count, seq_length), F32)
     dma = pltpu.SemaphoreType.DMA
     spec = pltpu.VMEM((bins, 2 * TILE, TILE), F32)
+    rows_like = jax.ShapeDtypeStruct((tokens, width), BF16)
     flops = 6 * bins * 2 * 2 * TILE * 2 * TILE * TILE
-    conv_out, conv_grad, filter_raw, factor = pl.pallas_call(
+    query_part, key_part, value_part, filter_raw, factor = pl.pallas_call(
         functools.partial(fused_kernel, (blocks, n_ctx, n_tp, entries)),
         out_shape=(
-            jax.ShapeDtypeStruct((tokens, width), BF16),
-            jax.ShapeDtypeStruct((tokens, width), BF16),
+            rows_like, rows_like, rows_like,
             jax.ShapeDtypeStruct((chan_count, seq_length), F32),
             jax.ShapeDtypeStruct((1, 1), F32),
         ),
         in_specs=[hbm] * 7,
-        out_specs=(hbm, hbm, hbm, vmem),
+        out_specs=(hbm, hbm, hbm, hbm, vmem),
         scratch_shapes=[
             stream, stream, stream, stream, lags, lags,
             pltpu.VMEM(fwd.shape, BF16),
@@ -588,7 +633,7 @@
             pltpu.VMEM((8, TILE), F32),
             pltpu.VMEM((blocks, 8, TILE), F32),
             dma((5, 4)),
-            dma((2, blocks)),
+            dma((3, blocks)),
             dma(()),
             dma((2,)),
             dma((4, blocks)),
@@ -599,7 +644,7 @@
             dma((max(n_tp - 1, 1),)),
         ],
         compiler_params=pltpu.CompilerParams(
-            collective_id=0, has_side_effects=True, vmem_limit_bytes=50 * 1024 * 1024
+            collective_id=0, has_side_effects=True, vmem_limit_bytes=VMEM_LIMIT
         ),
         cost_estimate=pl.CostEstimate(
             flops=flops, bytes_accessed=16 * tokens * width, transcendentals=0
@@ -609,10 +654,18 @@
         long_filter.reshape(chan_count, seq_length),
         jnp.asarray(fwd), jnp.asarray(inv),
     )
-    query_grad = gated_product(output_grad, conv_out)
-    key_grad = gated_product(conv_grad, value_proj)
-    value_grad = gated_product(conv_grad, key_proj)
-    filter_grad = (filter_raw * factor.reshape(())).reshape(1, chan_count, seq_length)
+    query_grad, key_grad, value_grad, filter_grad = pl.pallas_call(
+        finish_kernel,
+        out_shape=(rows_like,) * 3 + (jax.ShapeDtypeStruct((chan_count, seq_length), F32),),
+        in_specs=[hbm] * 4 + [vmem],
+        out_specs=(hbm,) * 4,
+        scratch_shapes=[lags, lags, dma((3, PARTS)), dma((PARTS,)), dma((PARTS,))],
+        compiler_params=pltpu.CompilerParams(vmem_limit_bytes=VMEM_LIMIT),
+        cost_estimate=pl.CostEstimate(
+            flops=tokens * width, bytes_accessed=20 * tokens * width, transcendentals=0
+        ),
+    )(query_part, key_part, value_part, filter_raw, factor)
+    filter_grad = filter_grad.reshape(1, chan_count, seq_length)
     return (query_grad, key_grad, value_grad, filter_grad)
 
 

time: 66.2 us -> 108 us (1.63)
  Pallas kernels: 57.8 us -> 108 us
  local copies, waits for them, and re-layouts: 4.16 us -> 0 us
  other arithmetic: 3.22 us -> 0 us
    pallas_call x0 -> x1, Pallas kernels: none -> 49.5 us  [fused_body(): pl.pallas_call(finish_kernel, out_shape=(rows_like,) * 3 + (jax.ShapeDtyp...]
    unnamed x10 -> x0, local copies, waits for them, and re-layouts: 4.16 us -> none
    reshape x1 -> x0, other arithmetic: 1.69 us -> none  [fused_body(): (filter_raw * factor.reshape(())).reshape(1, chan_count, seq_length)]
    convert_element_type x1 -> x0, other arithmetic: 1.52 us -> none  [gated_product(): (left.astype(jnp.float32) * right.astype(jnp.float32)).astype(jnp.bfloat16)]
where the time goes in v3:
time: 108 us
  Pallas kernels  108 us (100%)
    pallas_call x1, Pallas kernels, fused_body(): pl.pallas_call(functools.partial(fused_kernel, (blocks, n_ctx, n_tp, entr...  58.2 us
    pallas_call x1, Pallas kernels, fused_body(): pl.pallas_call(finish_kernel, out_shape=(rows_like,) * 3 + (jax.ShapeDtyp...  49.5 us

profile of v3, /device:TPU:0, one launch (start us, length us, event | category | flops | bytes accessed | tf_op | source)
XLA Modules:
  0.0 108.3 jit_solution(17524509939113528190)
XLA Ops:
  0.6 58.2 %shard_map.102 = (bf16[128,2048]{1,0:T(8,128)(2,1)}, bf16[128,2048]{1,0:T(8,128)(2,1)}, bf16[128,2048]{1,0:T(8,128)(2,1)}, f32[128,2048]{1,0:T(8,128)}, f32[1,1]{1,0:T(1,128)}) custom-call(bf16[128,2048]{1,0:T(8,128)(2,1)} %k_hbm.1, bf16[128,2048]{1,0:T(8,128)(2,1)} %v_hbm.1, bf16[128,2048]{1,0:T(8,128)(2,1)} %q_hbm.1, bf16[128,2048]{1,0:T(8,128)(2,1)} %og_hbm.1, ...), custom_call_target="tpu_custom_call" | custom-call | flops 1711276032 | bytes 4194304 | tf_op jit(solution)/shard_map/pallas_call | solution.py:613
  58.8 49.5 %shard_map.103 = (bf16[128,2048]{1,0:T(8,128)(2,1)}, bf16[128,2048]{1,0:T(8,128)(2,1)}, bf16[128,2048]{1,0:T(8,128)(2,1)}, f32[128,2048]{1,0:T(8,128)}) custom-call(bf16[128,2048]{1,0:T(8,128)(2,1)} %get-tuple-element.13.qg_in, bf16[128,2048]{1,0:T(8,128)(2,1)} %get-tuple-element.14.kg_in, bf16[128,2048]{1,0:T(8,128)(2,1)} %get-tuple-element.15.vg_in, ...), custom_call_target="tpu_custom_call" | custom-call | flops 262144 | bytes 5242880 | tf_op jit(solution)/shard_map/pallas_call | solution.py:657

commit v4 on v3

--- a/solution.py
+++ b/solution.py
@@ -318,18 +318,14 @@
             weight *= 2
         return out
 
-    def start_all(phase, after=None):
-        for mask in range(n_ctx - 1, -1, -1):
-            ctx = flipped(lax.axis_index("ctx"), mask)
-
-            def one(j, carry, ctx=ctx):
-                blk = lax.rem(lax.axis_index("blk") + j, blocks // n_ctx)
-                if after is not None:
-                    out_copy(after, blk * n_ctx + ctx).wait_send()
-                out_copy(phase, blk * n_ctx + ctx).start()
-                return carry
-
-            lax.fori_loop(0 if mask else 1, blocks // n_ctx, one, 0)
+    def start_all(phase):
+        masks = [m for pair in zip(range(n_ctx - 1, -1, -1), range(n_ctx)) for m in pair][:n_ctx]
+        ctxs = [(mask, flipped(lax.axis_index("ctx"), mask)) for mask in masks]
+        for j in range(blocks // n_ctx):
+            blk = lax.rem(lax.axis_index("blk") + j, blocks // n_ctx)
+            for mask, ctx in ctxs:
+                if j or mask:
+                    out_copy(phase, blk * n_ctx + ctx).start()
 
     def arrive_all(phase):
         def one(j, carry):
@@ -388,6 +384,7 @@
     pl.semaphore_wait(barrier, blocks - 1 + n_tp - 1)
     start_all(0)
     gate(1, og_ref, q_ref)
+    start_all(1)
 
     for part in range(4):
         load(4, part).wait()
@@ -412,7 +409,6 @@
             spec_f[k] = spec
 
     each_bin(filter_step)
-    start_all(1, after=0)
 
     arrive_all(0)
     outer_forward(lambda n, rows: recv[0, n, rows, :])
@@ -556,7 +552,7 @@
 
     def sent(j, carry):
         d = lax.rem(me + j, blocks)
-        for phase in range(1, 4):
+        for phase in range(4):
             out_copy(phase, d).wait_send()
         sq_out(d).wait_send()
         return carry
@@ -568,30 +564,28 @@
 
 def finish_kernel(
     qg_in, kg_in, vg_in, raw_hbm, fac_ref, qg_out, kg_out, vg_out, fg_hbm,
-    raw, fg, move_sem, load_sem, store_sem,
+    qg, kg, vg, raw, load_sem, store_sem,
 ):
     step = raw.shape[0] // PARTS
 
-    def copy(src, dst, sem, part):
+    def copy(src, dst, sems, i, part):
         rows = pl.ds(part * step, step)
-        return pltpu.make_async_copy(src.at[rows], dst.at[rows], sem)
-
-    loads = [copy(raw_hbm, raw, load_sem.at[p], p) for p in range(PARTS)]
-    stores = [copy(fg, fg_hbm, store_sem.at[p], p) for p in range(PARTS)]
-    moves = [
-        copy(src, dst, move_sem.at[i, p], p)
-        for p in range(PARTS)
-        for i, (src, dst) in enumerate(((qg_in, qg_out), (kg_in, kg_out), (vg_in, vg_out)))
-    ]
-    for item in loads + moves:
-        item.start()
-    for p in range(PARTS):
-        loads[p].wait()
-        rows = slice(p * step, (p + 1) * step)
-        fg[rows] = raw[rows] * fac_ref[...]
-        stores[p].start()
-    for item in moves + stores:
-        item.wait()
+        return pltpu.make_async_copy(src.at[rows], dst.at[rows], sems.at[i, part])
+
+    ways = ((raw_hbm, raw, fg_hbm), (qg_in, qg, qg_out), (kg_in, kg, kg_out), (vg_in, vg, vg_out))
+    for part in range(PARTS):
+        for i, (src, held, dst) in enumerate(ways):
+            copy(src, held, load_sem, i, part).start()
+    for part in range(PARTS):
+        for i, (src, held, dst) in enumerate(ways):
+            copy(src, held, load_sem, i, part).wait()
+            if i == 0:
+                rows = slice(part * step, (part + 1) * step)
+                raw[rows] = raw[rows] * fac_ref[...]
+            copy(held, dst, store_sem, i, part).start()
+    for part in range(PARTS):
+        for i, (src, held, dst) in enumerate(ways):
+            copy(held, dst, store_sem, i, part).wait()
 
 
 def fused_body(mesh, query_proj, key_proj, value_proj, output_grad, long_filter):
@@ -659,7 +653,7 @@
         out_shape=(rows_like,) * 3 + (jax.ShapeDtypeStruct((chan_count, seq_length), F32),),
         in_specs=[hbm] * 4 + [vmem],
         out_specs=(hbm,) * 4,
-        scratch_shapes=[lags, lags, dma((3, PARTS)), dma((PARTS,)), dma((PARTS,))],
+        scratch_shapes=[stream, stream, stream, lags, dma((4, PARTS)), dma((4, PARTS))],
         compiler_params=pltpu.CompilerParams(vmem_limit_bytes=VMEM_LIMIT),
         cost_estimate=pl.CostEstimate(
             flops=tokens * width, bytes_accessed=20 * tokens * width, transcendentals=0

time: 108 us -> 62.3 us (0.58)
  Pallas kernels: 108 us -> 61.5 us
    pallas_call x1, Pallas kernels: 49.5 us -> 3.38 us  [fused_body(): pl.pallas_call(finish_kernel, out_shape=(rows_like,) * 3 + (jax.ShapeDtyp...]
where the time goes in v4:
time: 62.3 us; the launch traced here: 62.1 us
  Pallas kernels  61.5 us (99%)
  between operations  0.64 us (1%)
    pallas_call x1, Pallas kernels, fused_body(): pl.pallas_call(functools.partial(fused_kernel, (blocks, n_ctx, n_tp, entr...  58.1 us
    pallas_call x1, Pallas kernels, fused_body(): pl.pallas_call(finish_kernel, out_shape=(rows_like,) * 3 + (jax.ShapeDtyp...  3.38 us

profile of v4, /device:TPU:0, one launch (start us, length us, event | category | flops | bytes accessed | tf_op | source)
XLA Modules:
  0.0 62.1 jit_solution(16487305321093706522)
XLA Ops:
  0.6 58.1 %shard_map.102 = (bf16[128,2048]{1,0:T(8,128)(2,1)}, bf16[128,2048]{1,0:T(8,128)(2,1)}, bf16[128,2048]{1,0:T(8,128)(2,1)}, f32[128,2048]{1,0:T(8,128)}, f32[1,1]{1,0:T(1,128)}) custom-call(bf16[128,2048]{1,0:T(8,128)(2,1)} %k_hbm.1, bf16[128,2048]{1,0:T(8,128)(2,1)} %v_hbm.1, bf16[128,2048]{1,0:T(8,128)(2,1)} %q_hbm.1, bf16[128,2048]{1,0:T(8,128)(2,1)} %og_hbm.1, ...), custom_call_target="tpu_custom_call" | custom-call | flops 1711276032 | bytes 4194304 | tf_op jit(solution)/shard_map/pallas_call | solution.py:607
  58.7 3.4 %shard_map.103 = (bf16[128,2048]{1,0:T(8,128)(2,1)}, bf16[128,2048]{1,0:T(8,128)(2,1)}, bf16[128,2048]{1,0:T(8,128)(2,1)}, f32[128,2048]{1,0:T(8,128)}) custom-call(bf16[128,2048]{1,0:T(8,128)(2,1)} %get-tuple-element.13.qg_in, bf16[128,2048]{1,0:T(8,128)(2,1)} %get-tuple-element.14.kg_in, bf16[128,2048]{1,0:T(8,128)(2,1)} %get-tuple-element.15.vg_in, ...), custom_call_target="tpu_custom_call" | custom-call | flops 262144 | bytes 5242880 | tf_op jit(solution)/shard_map/pallas_call | solution.py:651

commit v5 on v4

--- a/solution.py
+++ b/solution.py
@@ -340,12 +340,16 @@
     def outer_forward(load):
         def one(i, carry):
             rows = rows_at(i)
-            out = padded_bins([load(n, rows).astype(F32) for n in range(blocks)])
+            tiles = [load(n, rows).astype(F32) for n in range(blocks)]
+            halves = [padded_bins([t[h : h + 8] for t in tiles]) for h in (0, 8)]
             low = pl.ds(pl.multiple_of(TILE + i * CHUNK, CHUNK), CHUNK)
             for k in range(bins):
-                re, im = out[k]
-                outer[k, rows, :] = re.astype(BF16)
-                outer[k, low, :] = (jnp.zeros_like(re) if im is None else im).astype(BF16)
+                re, im = zip(*[half[k] for half in halves])
+                outer[k, rows, :] = jnp.concatenate(re, 0).astype(BF16)
+                if im[0] is None:
+                    outer[k, low, :] = jnp.zeros((CHUNK, TILE), BF16)
+                else:
+                    outer[k, low, :] = jnp.concatenate(im, 0).astype(BF16)
             return carry
 
         lax.fori_loop(0, TILE // CHUNK, one, 0)
@@ -363,10 +367,14 @@
     def outer_back(store):
         def one(i, carry):
             rows = rows_at(i)
-            low = pl.ds(pl.multiple_of(TILE + i * CHUNK, CHUNK), CHUNK)
-            got = {k: (back[k, rows, :], back[k, low, :]) for k in range(bins)}
-            for n, y in enumerate(padded_back(got, blocks)):
-                store(n, rows, y)
+            halves = []
+            for h in (0, 8):
+                top = pl.ds(pl.multiple_of(i * CHUNK + h, 8), 8)
+                low = pl.ds(pl.multiple_of(TILE + i * CHUNK + h, 8), 8)
+                got = {k: (back[k, top, :], back[k, low, :]) for k in range(bins)}
+                halves.append(padded_back(got, blocks))
+            for n, pair in enumerate(zip(*halves)):
+                store(n, rows, jnp.concatenate(pair, 0))
             return carry
 
         lax.fori_loop(0, TILE // CHUNK, one, 0)

time: 62.3 us -> 62.3 us (level)
  no operation moved by 1% of the time
where the time goes in v5:
time: 62.3 us; the launch traced here: 62.1 us
  Pallas kernels  61.5 us (99%)
  between operations  0.64 us (1%)
    pallas_call x1, Pallas kernels, fused_body(): pl.pallas_call(functools.partial(fused_kernel, (blocks, n_ctx, n_tp, entr...  58.1 us
    pallas_call x1, Pallas kernels, fused_body(): pl.pallas_call(finish_kernel, out_shape=(rows_like,) * 3 + (jax.ShapeDtyp...  3.38 us

profile of v5, /device:TPU:0, one launch (start us, length us, event | category | flops | bytes accessed | tf_op | source)
XLA Modules:
  0.0 62.1 jit_solution(17566897046073156312)
XLA Ops:
  0.6 58.1 %shard_map.102 = (bf16[128,2048]{1,0:T(8,128)(2,1)}, bf16[128,2048]{1,0:T(8,128)(2,1)}, bf16[128,2048]{1,0:T(8,128)(2,1)}, f32[128,2048]{1,0:T(8,128)}, f32[1,1]{1,0:T(1,128)}) custom-call(bf16[128,2048]{1,0:T(8,128)(2,1)} %k_hbm.1, bf16[128,2048]{1,0:T(8,128)(2,1)} %v_hbm.1, bf16[128,2048]{1,0:T(8,128)(2,1)} %q_hbm.1, bf16[128,2048]{1,0:T(8,128)(2,1)} %og_hbm.1, ...), custom_call_target="tpu_custom_call" | custom-call | flops 1711276032 | bytes 4194304 | tf_op jit(solution)/shard_map/pallas_call | solution.py:615
  58.7 3.4 %shard_map.103 = (bf16[128,2048]{1,0:T(8,128)(2,1)}, bf16[128,2048]{1,0:T(8,128)(2,1)}, bf16[128,2048]{1,0:T(8,128)(2,1)}, f32[128,2048]{1,0:T(8,128)}) custom-call(bf16[128,2048]{1,0:T(8,128)(2,1)} %get-tuple-element.13.qg_in, bf16[128,2048]{1,0:T(8,128)(2,1)} %get-tuple-element.14.kg_in, bf16[128,2048]{1,0:T(8,128)(2,1)} %get-tuple-element.15.vg_in, ...), custom_call_target="tpu_custom_call" | custom-call | flops 262144 | bytes 5242880 | tf_op jit(solution)/shard_map/pallas_call | solution.py:659
